TPU v7x, 32 devices: a whole 2x2x4 slice. The times are simulated.
32 devices in a mesh: slot: 4 (over x, core), horiz: 8 (over z, y).
Axes of the slice: x: 2, y: 2, z: 4, core: 2. Of those that a mesh axis runs over, the one named last changes fastest.
Arguments:
- control: bfloat16 [32, 80, 16, 128], P(None, None, 'horiz'), may hold values from -6 to 6
- land_mask: int32 [80, 16, 128], P(None, 'horiz'), may hold values 0 or 1
- tile_id: int32 [4, 32], replicated, may hold values from 0 to 15
- tile_scale: float32 [16, 80], replicated, may hold values from 0.3 to 3
- inverse_x: bfloat16 [128, 128], replicated
- inverse_y: bfloat16 [16, 16], replicated
- inverse_z: bfloat16 [80, 80], replicated
- perturbations: bfloat16 [4, 32, 80, 16, 128], P('slot', None, None, 'horiz'), may hold values from -6 to 6
- obs_cell: int32 [4, 65536], P('slot', 'horiz'), may hold values from 0 to 20479
- obs_value: float32 [4, 65536], P('slot', 'horiz'), may hold values from -6 to 6
- obs_weight: float32 [4, 65536], P('slot', 'horiz'), may hold values from 1 to 8
Outputs:
- gradient: bfloat16 [32, 80, 16, 128], P(None, None, 'horiz')
Inputs may be any that keep to these rules, and one draw needn't show every extreme that they name: obs_cell[s, j] indexes the cells of tile j // 8192 (rows j // 8192 * 2 onward), level-major, then row, then column.
All inputs are finite; a program needn't handle non-finite values. No bound on the sum of `land_mask` on one device may be relied on, other than what follows from the above.
Results may differ from a plain program's by a relative error of at most 0.006.
Values may be sent and summed in bfloat16 or wider, within the bound.
A program may use at most 192 MiB of HBM per device.

v0:
```python
import math

import jax
import jax.numpy as jnp
from jax import lax
from jax.sharding import PartitionSpec as P


def local_sigma(tile_id, tile_scale, dev_index, row_count):
    regions = tile_scale.shape[0]
    tile_rows = max(row_count // 4, 1)
    picked = lax.dynamic_slice_in_dim(tile_id, dev_index * row_count // 4, tile_rows, 0)
    onehot = (picked[None] == jnp.arange(regions, dtype=jnp.int32)[:, None, None]).astype(
        jnp.float32
    )
    scale_table = jnp.einsum("rz,rab->zab", tile_scale, onehot, precision=lax.Precision.HIGHEST)
    expanded = jnp.repeat(scale_table, 4, axis=1)
    expanded = lax.dynamic_slice_in_dim(expanded, dev_index * row_count % 4, row_count, 1)
    return jnp.repeat(expanded, 4, axis=2)


def columns_filter(received, inverse_y, inverse_z):
    across = jnp.einsum(
        "mzyx,yk->mzkx", received, inverse_y, preferred_element_type=jnp.float32
    ).astype(jnp.bfloat16)
    return jnp.einsum(
        "mzyx,zk->mkyx", across, inverse_z, preferred_element_type=jnp.float32
    ).astype(jnp.bfloat16)


def forward_filter(control, sea_mask, mask_half, weight_mask, inverse_x, inverse_y, inverse_z):
    masked = (weight_mask * control.astype(jnp.float32)).astype(jnp.bfloat16)
    along_x = (sea_mask * jnp.dot(masked, inverse_x, preferred_element_type=jnp.float32)).astype(
        jnp.bfloat16
    )
    deeper = columns_filter(
        lax.all_to_all(along_x, "horiz", split_axis=3, concat_axis=2, tiled=True),
        inverse_y,
        inverse_z,
    )
    returned = lax.all_to_all(deeper, "horiz", split_axis=2, concat_axis=3, tiled=True)
    return returned * mask_half


def adjoint_filter(slot_sum, sea_mask, weight_mask, inverse_x, inverse_y, inverse_z):
    back_first = (sea_mask * slot_sum).astype(jnp.bfloat16)
    back_deep = jnp.einsum(
        "mkyx,zk->mzyx",
        lax.all_to_all(back_first, "horiz", split_axis=3, concat_axis=2, tiled=True),
        inverse_z,
        preferred_element_type=jnp.float32,
    ).astype(jnp.bfloat16)
    back_across = jnp.einsum(
        "mzkx,yk->mzyx", back_deep, inverse_y, preferred_element_type=jnp.float32
    ).astype(jnp.bfloat16)
    returned = lax.all_to_all(back_across, "horiz", split_axis=2, concat_axis=3, tiled=True)
    along_x = lax.dot_general(
        returned * sea_mask.astype(jnp.bfloat16),
        inverse_x,
        (((3,), (1,)), ((), ())),
        preferred_element_type=jnp.float32,
    )
    return weight_mask * along_x


def observe(increment, cells, values, weights):
    flat_inc = increment.reshape(-1)
    misfit = weights * (flat_inc[cells] - values)
    return jnp.zeros(flat_inc.shape, jnp.float32).at[cells].add(misfit).reshape(increment.shape)


def per_device(
    control,
    land_mask,
    tile_id,
    tile_scale,
    inverse_x,
    inverse_y,
    inverse_z,
    perturbations,
    obs_cell,
    obs_value,
    obs_weight,
):
    members, levels, row_count, col_count = control.shape
    dev_index = lax.axis_index("horiz")
    sea_mask = land_mask.astype(jnp.float32)
    mask_half = land_mask.astype(jnp.bfloat16)
    weight_mask = sea_mask * local_sigma(tile_id, tile_scale, dev_index, row_count)
    spread_w = forward_filter(
        control, sea_mask, mask_half, weight_mask, inverse_x, inverse_y, inverse_z
    )
    norm_scale = 1.0 / math.sqrt(members)
    perturbed = perturbations[0]
    increment = (
        jnp.einsum("mzyx,mzyx->zyx", perturbed, spread_w, preferred_element_type=jnp.float32)
        * norm_scale
    )
    adjoint_obs = observe(increment, obs_cell[0], obs_value[0], obs_weight[0])
    summed = perturbed * (adjoint_obs * norm_scale)[None]
    slot_sum = lax.psum(summed.astype(jnp.bfloat16), "slot").astype(jnp.float32)
    filtered = adjoint_filter(slot_sum, sea_mask, weight_mask, inverse_x, inverse_y, inverse_z)
    gradient = (control.astype(jnp.float32) + filtered).astype(jnp.bfloat16)
    return gradient


def solution(mesh):
    return jax.shard_map(
        per_device,
        mesh=mesh,
        in_specs=(
            P(None, None, "horiz", None),
            P(None, "horiz", None),
            P(),
            P(),
            P(),
            P(),
            P(),
            P("slot", None, None, "horiz", None),
            P("slot", "horiz"),
            P("slot", "horiz"),
            P("slot", "horiz"),
        ),
        out_specs=P(None, None, "horiz", None),
        check_vma=False,
    )
```

profile of v0, /device:TPU:0, one launch (start us, length us, event | category | flops | bytes accessed | tf_op | source)
XLA Modules:
  0.0 399.7 jit_solution(14885990398787739606)
XLA Ops:
  6.5 0.7 dynamic-slice_bitcast_fusion
  7.2 0.9 convolution_bitcast_fusion
  8.2 0.1 copy.37
  8.2 1.7 convert_convert_fusion
  9.9 0.9 broadcast_multiply_fusion.2
  10.9 0.6 copy-done.3
  11.5 1.8 multiply_convert_fusion.2
  13.3 3.6 copy.41
  16.9 55.3 %all_to_all.72 = bf16[32,80,2,128]{1,2,0,3:T(2,128)(2,1)S(1)} all-to-all(bf16[32,80,2,128]{1,2,0,3:T(2,128)(2,1)S(1)} %copy.41), channel_id=1, replica_groups=mesh['slot'=4,'horiz'=8] {'horiz'}, dimensions={3} | all-to-all | bytes 2621440 | tf_op jit(solution)/shard_map/all_to_all | solution.py:37
  72.2 2.4 copy.42
  74.7 0.0 copy-start.11
  74.7 0.4 copy.43
  75.1 0.2 copy-done.11
  75.4 0.8 convert_bitcast_fusion.2
  76.1 0.0 copy-done.7
  76.1 3.8 convert_bitcast_fusion.1
  79.9 3.7 all-to-all-start.1
  83.7 0.0 all-reduce.2.cloned.1.call-start
  83.7 0.1 copy.48
  83.9 47.6 %all-to-all-done.1 = bf16[32,80,16,16]{1,0,3,2:T(8,128)(2,1)S(1)} async-done(((bf16[32,80,16,16]{1,0,3,2:T(8,128)(2,1)}), bf16[32,80,16,16]{1,0,3,2:T(8,128)(2,1)S(1)}, u32[]{:S(2)}, u32[]{:S(2)}) %all-to-all-start.1) | async-done | bytes 1310752 | tf_op jit(solution)/shard_map/all_to_all | solution.py:41
  131.5 0.8 copy.47
  132.3 2.4 bitcast_convert_fusion
  134.7 3.9 copy.67
  138.6 1.6 multiply_reduce_fusion
  140.2 0.0 copy-start.9
  140.2 0.0 copy-start.10
  140.3 0.0 copy-start.1
  140.3 45.5 %gather_fusion = f32[8192]{0:T(1024)S(1)} fusion(f32[20480]{0:T(1024)S(1)} %bitcast.76, s32[8192]{0:T(1024)S(1)} %broadcast_clamp_fusion), kind=kCustom, calls=%fused_computation | custom fusion | bytes 98304 | tf_op jit(solution)/shard_map/gather | solution.py:68
  185.8 43.4 %scatter_custom_fusion = f32[20480]{0:T(1024)S(1)} fusion(s32[8192]{0:T(1024)S(1)} %bitcast.86, f32[8192]{0:T(1024)S(1)} %subtract_multiply_fusion, f32[]{:T(128)} %constant.32.clone.1), kind=kCustom, calls=%fused_computation.31 | custom fusion | flops 8192 | bytes 81924 | tf_op jit(solution)/shard_map/scatter-add | solution.py:69
  229.3 1.3 multiply_convert_fusion.1
  230.6 0.0 all-reduce.2.cloned.1.call-update
  230.6 38.1 %all-reduce.2.cloned.1.call-done = bf16[32,80,2,128]{3,1,2,0:T(8,128)(2,1)} async-done(((bf16[32,80,2,128]{3,1,2,0:T(8,128)(2,1)}), bf16[32,80,2,128]{3,1,2,0:T(8,128)(2,1)}) %all-reduce.2.cloned.1.call-update) | async-done | bytes 1310736 | tf_op jit(solution)/shard_map/psum | solution.py:101
  268.8 1.6 multiply_convert_fusion
  270.3 3.6 copy.50
  273.9 53.6 %all_to_all.73 = bf16[32,80,2,128]{1,2,0,3:T(2,128)(2,1)S(1)} all-to-all(bf16[32,80,2,128]{1,2,0,3:T(2,128)(2,1)S(1)} %copy.50), channel_id=1, replica_groups=mesh['slot'=4,'horiz'=8] {'horiz'}, dimensions={3} | all-to-all | bytes 2621440 | tf_op jit(solution)/shard_map/all_to_all | solution.py:49
  327.5 2.4 copy.51
  329.9 0.4 copy.52
  330.4 2.7 convert_bitcast_fusion
  333.0 3.5 copy.54
  336.5 3.7 all-to-all-start.3
  340.2 0.1 copy.56
  340.4 47.7 %all-to-all-done.3 = bf16[32,80,16,16]{1,3,0,2:T(8,128)(2,1)S(1)} async-done(((bf16[32,80,16,16]{1,3,0,2:T(8,128)(2,1)}), bf16[32,80,16,16]{1,3,0,2:T(8,128)(2,1)S(1)}, u32[]{:S(2)}, u32[]{:S(2)}) %all-to-all-start.3) | async-done | bytes 1310752 | tf_op jit(solution)/shard_map/all_to_all | solution.py:56
  388.1 0.6 copy.55
  388.7 0.0 copy-start.2
  388.7 0.3 bitcast_multiply_fusion
  389.0 1.0 copy-done.2
  390.0 0.7 fusion.1
  390.8 2.1 copy.58
  (25 shorter events, 0.2 us)
Async XLA Ops:
  6.5 5.0 %copy-start = (bf16[128,128]{1,0:T(8,128)(2,1)S(1)}, bf16[128,128]{1,0:T(8,128)(2,1)}, u32[]{:S(2)}) copy-start(bf16[128,128]{1,0:T(8,128)(2,1)} %param.15) | copy-start | bytes 98308
  10.9 0.6 copy-start.3
  74.7 0.7 copy-start.11
  75.4 0.8 copy-start.7
  79.9 3.8 copy-start.6
  79.9 3.9 copy-start.8
  79.9 51.6 %all-to-all-start.1 = ((bf16[32,80,16,16]{1,0,3,2:T(8,128)(2,1)}), bf16[32,80,16,16]{1,0,3,2:T(8,128)(2,1)S(1)}, u32[]{:S(2)}, u32[]{:S(2)}) async-start(bf16[32,80,16,16]{1,0,3,2:T(8,128)(2,1)} %convert_bitcast_fusion.1), calls=%async_computation.1 | async-start | bytes 4194304 | tf_op jit(solution)/shard_map/all_to_all | solution.py:41
  83.7 185.1 %all-reduce.2.cloned.1.call-start = ((), (), s32[]{:S(2)}) async-start(), calls=%async_computation.4 | async-start | bytes 2621440 | tf_op jit(solution)/shard_map/psum | solution.py:101
  140.2 45.6 %copy-start.9 = (f32[1,8192]{1,0:T(1,128)S(1)}, f32[1,8192]{1,0:T(1,128)}, u32[]{:S(2)}) copy-start(f32[1,8192]{1,0:T(1,128)} %param.21) | copy-start | bytes 98308
  140.2 45.6 %copy-start.10 = (f32[1,8192]{1,0:T(1,128)S(1)}, f32[1,8192]{1,0:T(1,128)}, u32[]{:S(2)}) copy-start(f32[1,8192]{1,0:T(1,128)} %param.20) | copy-start | bytes 98308
  140.3 89.0 %copy-start.1 = (bf16[1,32,80,2,128]{4,3,2,1,0:T(2,128)(2,1)S(1)}, bf16[1,32,80,2,128]{4,3,2,1,0:T(2,128)(2,1)}, u32[]{:S(2)}) copy-start(bf16[1,32,80,2,128]{4,3,2,1,0:T(2,128)(2,1)} %param.18) | copy-start | bytes 3932164
  229.2 39.5 %copy-start.4 = (f32[80,2,128]{2,0,1:T(8,128)S(1)}, f32[80,2,128]{2,0,1:T(8,128)}, u32[]{:S(2)}) copy-start(f32[80,2,128]{2,0,1:T(8,128)} %copy-done.3) | copy-start | bytes 245764
  336.5 3.7 copy-start.5
  336.5 51.6 %all-to-all-start.3 = ((bf16[32,80,16,16]{1,3,0,2:T(8,128)(2,1)}), bf16[32,80,16,16]{1,3,0,2:T(8,128)(2,1)S(1)}, u32[]{:S(2)}, u32[]{:S(2)}) async-start(bf16[32,80,16,16]{1,3,0,2:T(8,128)(2,1)} %copy.54), calls=%async_computation.3 | async-start | bytes 4194304 | tf_op jit(solution)/shard_map/all_to_all | solution.py:56
  388.7 1.3 copy-start.2
Sparse Core Ops, SparseCore 0:
  230.7 37.9 all-reduce.1
where the time goes:
time: 401 us; the launch traced here: 400 us
  waiting for transfers between devices  134 us (33%)
  blocking collectives  109 us (27%)
  local copies, waits for them, and re-layouts  72.2 us (18%)
  other arithmetic  53.2 us (13%)
  between operations  13.7 us (3%)
  matrix products  10.6 us (3%)
  starting transfers between devices  7.51 us (2%)
    all_to_all x1, blocking collectives, forward_filter(): lax.all_to_all(along_x, 'horiz', split_axis=3, concat_axis=2, tiled=True)  55.3 us
    all_to_all x1, blocking collectives, adjoint_filter(): lax.all_to_all(back_first, 'horiz', split_axis=3, concat_axis=2, tiled=True)  53.6 us
    all_to_all x1, waiting for transfers between devices, adjoint_filter(): lax.all_to_all(back_across, 'horiz', split_axis=2, concat_axis=3, tiled=T...  47.7 us
    all_to_all x1, waiting for transfers between devices, forward_filter(): lax.all_to_all(deeper, 'horiz', split_axis=2, concat_axis=3, tiled=True)  47.6 us
    gather x1, local copies, waits for them, and re-layouts, observe(): misfit = weights * (flat_inc[cells] - values)  45.5 us
    scatter-add x1, other arithmetic, observe(): jnp.zeros(flat_inc.shape, jnp.float32).at[cells].add(misfit)  43.4 us
    psum x1, waiting for transfers between devices, per_device(): slot_sum = lax.psum(summed.astype(jnp.bfloat16), 'slot').astype(jnp.float32)  38.1 us
  transfers between devices with their start and end apart: 3, of which 3 were waited for; matrix products, arithmetic and copies ran while one was open for 0% of the time, Pallas kernels for 0%

commit v1 on v0

v1 whole, which is shorter than its diff:
```python
import functools
import math

import jax
import jax.numpy as jnp
from jax import lax
from jax.experimental import pallas as pl
from jax.experimental.pallas import tpu as pltpu
from jax.sharding import PartitionSpec as P

LANES = 128
GROUP = 16
F32 = jnp.float32
BF16 = jnp.bfloat16
MESH = pl.DeviceIdType.MESH


def dot(a, b, ca=1, cb=0, precision=None):
    return lax.dot_general(
        a, b, (((ca,), (cb,)), ((), ())), preferred_element_type=F32, precision=precision
    )


def iota(shape, dim):
    return lax.broadcasted_iota(jnp.int32, shape, dim)


def spread_matrix(shape, index):
    return jnp.where(index == iota(shape, 1), 1.0, 0.0).astype(BF16)


def kernel(
    slots,
    tiles,
    rows,
    control,
    land,
    tile_id,
    tile_scale,
    inv_x,
    inv_y,
    inv_z,
    pert,
    cells,
    values,
    weights,
    out,
    sea,
    weight,
    ky,
    ky_t,
    kz,
    kz_t,
    obs_acc,
    inc,
    adj,
    send_a,
    recv_a,
    across,
    send_b,
    spread,
    stage_c,
    recv_c,
    stage_x,
    recv_x,
    stage_d,
    recv_d,
    deep,
    stage_e,
    recv_e,
    tile_ss,
    tile_rs,
    gather_ss,
    gather_rs,
    red_ss,
    red_rs,
):
    members, depth, cols = control.shape
    own = members // slots
    blocks = cols // LANES
    levels = depth // rows
    s = lax.axis_index("slot")
    h = lax.axis_index("horiz")
    sib = s + 1 - 2 * lax.rem(s, 2)
    far = s + 2 - 4 * (s // 2)
    diag = sib + 2 - 4 * (sib // 2)

    barrier = pltpu.get_barrier_semaphore()
    for d in range(1, tiles):
        pl.semaphore_signal(
            barrier, inc=1, device_id={"horiz": lax.rem(h + d, tiles)}, device_id_type=MESH
        )
    for peer in (sib, far):
        pl.semaphore_signal(barrier, inc=1, device_id={"slot": peer}, device_id_type=MESH)

    region = tile_id[pl.ds(h * rows // 4, 1), :].astype(F32).astype(BF16)
    blocks_x = tile_id.shape[1]
    widen = jnp.where(iota((blocks_x, cols), 1) // 4 == iota((blocks_x, cols), 0), 1.0, 0.0)
    region_x = dot(region, widen.astype(BF16))
    regions = tile_scale.shape[0]
    onehot = jnp.where(
        iota((regions, cols), 0).astype(F32) == region_x, 1.0, 0.0
    )
    to_level = spread_matrix((depth, levels), iota((depth, levels), 0) // rows)
    scale_rows = dot(
        to_level.astype(F32), tile_scale[...], 1, 1, precision=lax.Precision.HIGHEST
    )
    sea[...] = land[...].astype(F32)
    weight[...] = sea[...] * dot(scale_rows, onehot, precision=lax.Precision.HIGHEST)

    def at_block(ref, c):
        if blocks == 1:
            return ref[...]
        return ref[:, pl.ds(pl.multiple_of(c * LANES, LANES), LANES)]

    def member_block(ref, m, c):
        if blocks == 1:
            return ref[m]
        return ref[m, :, pl.ds(pl.multiple_of(c * LANES, LANES), LANES)]

    def to_tile(phase, d, src, dst):
        return pltpu.make_async_remote_copy(
            src_ref=src,
            dst_ref=dst,
            send_sem=tile_ss.at[phase, d],
            recv_sem=tile_rs.at[phase, d],
            device_id={"horiz": lax.rem(h + d, tiles)},
            device_id_type=MESH,
        )

    def to_slot(ss, rs, phase, d, src, dst, peer):
        return pltpu.make_async_remote_copy(
            src_ref=src,
            dst_ref=dst,
            send_sem=ss.at[phase, d],
            recv_sem=rs.at[phase, d],
            device_id={"slot": peer},
            device_id_type=MESH,
        )

    order = list(range(1, tiles)) + [0]

    first = []
    for d in order:
        u = lax.rem(h + d, tiles)
        k, c = u // blocks, lax.rem(u, blocks)
        masked = (weight[...] * control[s * own + k].astype(F32)).astype(BF16)
        along = (at_block(sea, c) * dot(masked, at_block(inv_x, c))).astype(BF16)
        if d == 0:
            recv_a[h] = along
        else:
            send_a[u] = along
            if d == 1:
                pl.semaphore_wait(barrier, tiles - 1 + 2)
            copy = to_tile(0, d, send_a.at[u], recv_a.at[h])
            copy.start()
            first.append(copy)

    wide = tiles * GROUP
    side = tiles * rows
    pos = iota((wide, side), 0)
    pick_y = spread_matrix((wide, side), pos // GROUP * rows + lax.rem(pos, rows))
    row_i, col_i = iota((wide, wide), 0), iota((wide, wide), 1)
    same = lax.rem(row_i, GROUP) // rows == lax.rem(col_i, GROUP) // rows
    half = dot(pick_y, inv_y[...]).astype(BF16)
    ky[...] = jnp.where(same, dot(half, pick_y, 1, 1), 0.0).astype(BF16)
    half = dot(pick_y, inv_y[...], 1, 1).astype(BF16)
    ky_t[...] = jnp.where(same, dot(half, pick_y, 1, 1), 0.0).astype(BF16)
    same = lax.rem(iota((depth, depth), 0), rows) == lax.rem(iota((depth, depth), 1), rows)
    half = dot(to_level, inv_z[...]).astype(BF16)
    kz[...] = jnp.where(same, dot(half, to_level, 1, 1), 0.0).astype(BF16)
    half = dot(to_level, inv_z[...], 1, 1).astype(BF16)
    kz_t[...] = jnp.where(same, dot(half, to_level, 1, 1), 0.0).astype(BF16)

    def filter_y(matrix, src, dst):
        for g in range(depth // GROUP):
            part = src[:, g * GROUP : (g + 1) * GROUP, :].reshape(wide, LANES)
            dst[:, g * GROUP : (g + 1) * GROUP, :] = (
                dot(matrix[...], part).astype(BF16).reshape(tiles, GROUP, LANES)
            )

    for copy in first:
        copy.wait_recv()
    filter_y(ky_t, recv_a, across)
    second = []
    for d in order:
        u = lax.rem(h + d, tiles)
        deeper = dot(kz_t[...], across[u]).astype(BF16)
        if d == 0:
            spread[s * tiles + h] = deeper
        else:
            send_b[u] = deeper
            copy = to_tile(1, d, send_b.at[u], spread.at[s * tiles + h])
            copy.start()
            second.append(copy)

    count = cells.shape[1]
    step = min(1024, count)
    shift = cols.bit_length() - 1
    obs_acc[...] = jnp.zeros_like(obs_acc)

    def observe(i, carry):
        where = pl.ds(pl.multiple_of(i * step, step), step)
        cell, w = cells[:, where], weights[:, where]
        wv = w * values[:, where]
        w_hi = w.astype(BF16).astype(F32)
        v_hi = wv.astype(BF16).astype(F32)
        on_row = jnp.where(iota((depth, step), 0) == (cell >> shift), 1.0, 0.0).astype(BF16)
        on_col = iota((cols, step), 0) == (cell & (cols - 1))
        parts = [
            jnp.where(on_col, part, 0.0).astype(BF16) for part in (w_hi, w - w_hi, v_hi, wv - v_hi)
        ]
        for n, part in enumerate(parts):
            obs_acc[n // 2] += dot(on_row, part, 1, 1)
        return carry

    lax.fori_loop(0, count // step, observe, 0)

    inc[...] = jnp.zeros_like(inc)

    def add_member(slot, unit):
        k, c = unit // blocks, lax.rem(unit, blocks)
        term = (
            member_block(pert, slot * own + k, c).astype(F32)
            * spread[slot * tiles + unit].astype(F32)
        )
        if blocks == 1:
            inc[...] += term
        else:
            inc[:, pl.ds(pl.multiple_of(c * LANES, LANES), LANES)] += term

    def source(d):
        return lax.rem(h - d + tiles, tiles)

    def gather_copy(phase, d, unit, peer, buf):
        return to_slot(gather_ss, gather_rs, phase, d, buf.at[unit], buf.at[unit], peer)

    arrive = [0] + list(range(1, tiles))
    core1, far1, fwd1 = [], [], []
    for d in arrive:
        if d > 0:
            second[d - 1].wait_recv()
        unit = s * tiles + source(d)
        far1.append(gather_copy(1, d, unit, far, spread))
        far1[-1].start()
        core1.append(gather_copy(0, d, unit, sib, spread))
        core1[-1].start()
        add_member(s, source(d))
    for d in arrive:
        far1[d].wait_recv()
        fwd1.append(gather_copy(2, d, far * tiles + source(d), sib, spread))
        fwd1[-1].start()
        add_member(far, source(d))
    for d in arrive:
        core1[d].wait_recv()
        add_member(sib, source(d))
    for d in arrive:
        fwd1[d].wait_recv()
        add_member(diag, source(d))

    norm = 1.0 / math.sqrt(members)
    adj[...] = sea[...] * ((inc[...] * norm * obs_acc[0] - obs_acc[1]) * norm)

    def partial(slot, u):
        k, c = u // blocks, lax.rem(u, blocks)
        return member_block(pert, slot * own + k, c).astype(F32) * at_block(adj, c)

    core2, near2, far2 = [], [], []
    for d in order:
        u = lax.rem(h + d, tiles)
        stage_c[u] = partial(diag, u).astype(BF16)
        core2.append(to_slot(red_ss, red_rs, 0, d, stage_c.at[u], recv_c.at[u], sib))
        core2[-1].start()
    for d in order:
        u = lax.rem(h + d, tiles)
        stage_c[tiles + u] = partial(sib, u).astype(BF16)
        near2.append(
            to_slot(red_ss, red_rs, 1, d, stage_c.at[tiles + u], recv_c.at[tiles + u], sib)
        )
        near2[-1].start()
    for n, d in enumerate(order):
        u = lax.rem(h + d, tiles)
        core2[n].wait_recv()
        stage_x[u] = (partial(far, u) + recv_c[u].astype(F32)).astype(BF16)
        far2.append(to_slot(red_ss, red_rs, 2, d, stage_x.at[u], recv_x.at[u], far))
        far2[-1].start()
    third = []
    for n, d in enumerate(order):
        u = lax.rem(h + d, tiles)
        near2[n].wait_recv()
        far2[n].wait_recv()
        total = partial(s, u) + recv_c[tiles + u].astype(F32) + recv_x[u].astype(F32)
        if d == 0:
            recv_d[h] = total.astype(BF16)
        else:
            stage_d[u] = total.astype(BF16)
            copy = to_tile(2, d, stage_d.at[u], recv_d.at[h])
            copy.start()
            third.append(copy)

    for d in arrive:
        if d > 0:
            third[d - 1].wait_recv()
        deep[source(d)] = dot(kz[...], recv_d[source(d)]).astype(BF16)
    filter_y(ky, deep, stage_e)
    fourth = []
    for d in order:
        u = lax.rem(h + d, tiles)
        if d == 0:
            recv_e[h] = stage_e[h]
        else:
            copy = to_tile(3, d, stage_e.at[u], recv_e.at[h])
            copy.start()
            fourth.append(copy)

    if blocks > 1:
        for copy in fourth:
            copy.wait_recv()
    core3, far3, fwd3 = [], [], []
    for n in range(own):
        if blocks == 1:
            if n > 0:
                fourth[n - 1].wait_recv()
            k = source(n)
            field = recv_e[k]
        else:
            k = n
            field = jnp.concatenate([recv_e[n * blocks + c] for c in range(blocks)], axis=1)
        field = (field.astype(F32) * sea[...]).astype(BF16)
        m = s * own + k
        out[m] = (
            control[m].astype(F32) + weight[...] * dot(field, inv_x[...], 1, 1)
        ).astype(BF16)
        far3.append(gather_copy(4, n, m, far, out))
        far3[-1].start()
        core3.append(gather_copy(3, n, m, sib, out))
        core3[-1].start()
    for n in range(own):
        k = source(n) if blocks == 1 else n
        far3[n].wait_recv()
        fwd3.append(gather_copy(5, n, far * own + k, sib, out))
        fwd3[-1].start()
    for n in range(own):
        core3[n].wait_recv()
        fwd3[n].wait_recv()
    for copy in (
        first + second + third + fourth + core1 + far1 + fwd1 + core2 + near2 + far2 + core3
        + far3 + fwd3
    ):
        copy.wait_send()


def per_device(
    slots,
    tiles,
    control,
    land_mask,
    tile_id,
    tile_scale,
    inverse_x,
    inverse_y,
    inverse_z,
    perturbations,
    obs_cell,
    obs_value,
    obs_weight,
):
    members, levels, rows, cols = control.shape
    depth = levels * rows
    blocks = cols // LANES
    assert slots == 4 and cols % LANES == 0 and cols & (cols - 1) == 0
    assert members // slots * blocks == tiles and depth % GROUP == 0 and 4 % rows == 0
    unit = (depth, LANES)
    vmem = pl.BlockSpec(memory_space=pltpu.VMEM)
    gradient = pl.pallas_call(
        functools.partial(kernel, slots, tiles, rows),
        out_shape=jax.ShapeDtypeStruct((members, depth, cols), BF16),
        in_specs=[vmem] * 11,
        out_specs=vmem,
        scratch_shapes=[
            pltpu.VMEM((depth, cols), F32),
            pltpu.VMEM((depth, cols), F32),
            pltpu.VMEM((tiles * GROUP, tiles * GROUP), BF16),
            pltpu.VMEM((tiles * GROUP, tiles * GROUP), BF16),
            pltpu.VMEM((depth, depth), BF16),
            pltpu.VMEM((depth, depth), BF16),
            pltpu.VMEM((2, depth, cols), F32),
            pltpu.VMEM((depth, cols), F32),
            pltpu.VMEM((depth, cols), F32),
            pltpu.VMEM((tiles,) + unit, BF16),
            pltpu.VMEM((tiles,) + unit, BF16),
            pltpu.VMEM((tiles,) + unit, BF16),
            pltpu.VMEM((tiles,) + unit, BF16),
            pltpu.VMEM((slots * tiles,) + unit, BF16),
            pltpu.VMEM((2 * tiles,) + unit, BF16),
            pltpu.VMEM((2 * tiles,) + unit, BF16),
            pltpu.VMEM((tiles,) + unit, BF16),
            pltpu.VMEM((tiles,) + unit, BF16),
            pltpu.VMEM((tiles,) + unit, BF16),
            pltpu.VMEM((tiles,) + unit, BF16),
            pltpu.VMEM((tiles,) + unit, BF16),
            pltpu.VMEM((tiles,) + unit, BF16),
            pltpu.VMEM((tiles,) + unit, BF16),
            pltpu.SemaphoreType.DMA((4, tiles)),
            pltpu.SemaphoreType.DMA((4, tiles)),
            pltpu.SemaphoreType.DMA((6, tiles)),
            pltpu.SemaphoreType.DMA((6, tiles)),
            pltpu.SemaphoreType.DMA((3, tiles)),
            pltpu.SemaphoreType.DMA((3, tiles)),
        ],
        compiler_params=pltpu.CompilerParams(
            collective_id=0, has_side_effects=True, vmem_limit_bytes=56 * 1024 * 1024
        ),
    )(
        control.reshape(members, depth, cols),
        land_mask.reshape(depth, cols),
        tile_id,
        tile_scale,
        inverse_x,
        inverse_y,
        inverse_z,
        perturbations.reshape(members, depth, cols),
        obs_cell,
        obs_value,
        obs_weight,
    )
    return gradient.reshape(members, levels, rows, cols)


def solution(mesh):
    return jax.shard_map(
        functools.partial(per_device, mesh.shape["slot"], mesh.shape["horiz"]),
        mesh=mesh,
        in_specs=(
            P(None, None, "horiz", None),
            P(None, "horiz", None),
            P(),
            P(),
            P(),
            P(),
            P(),
            P("slot", None, None, "horiz", None),
            P("slot", "horiz"),
            P("slot", "horiz"),
            P("slot", "horiz"),
        ),
        out_specs=P(None, None, "horiz", None),
        check_vma=False,
    )
```

time: 401 us -> 63.4 us (0.16)
  waiting for transfers between devices: 134 us -> 0 us
  blocking collectives: 109 us -> 0 us
  local copies, waits for them, and re-layouts: 72.2 us -> 3.27 us
  Pallas kernels: 0 us -> 59.9 us
  other arithmetic: 53.2 us -> 0 us
  between operations: 13.7 us -> 0.01 us
  matrix products: 10.6 us -> 0 us
  starting transfers between devices: 7.51 us -> 0 us
    all_to_all x2 -> x0, blocking collectives: 109 us -> none  [the longest x1 55.3 us: forward_filter(): lax.all_to_all(along_x, 'horiz', split_axis=3, concat_axis=2, tiled=True)]
    all_to_all x2 -> x0, waiting for transfers between devices: 95.3 us -> none  [the longest x1 47.7 us: adjoint_filter(): lax.all_to_all(back_across, 'horiz', split_axis=2, concat_axis=3, tiled=T...]
    pallas_call x0 -> x1, Pallas kernels: none -> 59.9 us  [per_device(): pl.pallas_call(functools.partial(kernel, slots, tiles, rows), out_shape=j...]
    gather x1 -> x0, local copies, waits for them, and re-layouts: 45.5 us -> none  [observe(): misfit = weights * (flat_inc[cells] - values)]
    scatter-add x1 -> x0, other arithmetic: 43.4 us -> none  [observe(): jnp.zeros(flat_inc.shape, jnp.float32).at[cells].add(misfit)]
    psum x1 -> x0, waiting for transfers between devices: 38.1 us -> none  [per_device(): slot_sum = lax.psum(summed.astype(jnp.bfloat16), 'slot').astype(jnp.float32)]
    convert_element_type x7 -> x0, local copies, waits for them, and re-layouts: 13 us -> none  [the longest x1 3.6 us: adjoint_filter(): back_first = (sea_mask * slot_sum).astype(jnp.bfloat16)]
    dot_general x6 -> x0, matrix products: 10.6 us -> none  [the longest x1 3.77 us: columns_filter(): jnp.einsum('mzyx,zk->mkyx', across, inverse_z, preferred_element_type=jnp...]
  transfers between devices with their start and end apart: 3 -> 0, of which waited for: 3 -> 0; matrix products, arithmetic and copies ran while one was open for 0% -> 0% of each run, Pallas kernels for 0% -> 0%
where the time goes in v1:
time: 63.4 us; the launch traced here: 63.2 us
  Pallas kernels  59.9 us (94%)
  local copies, waits for them, and re-layouts  3.27 us (5%)
    pallas_call x1, Pallas kernels, per_device(): pl.pallas_call(functools.partial(kernel, slots, tiles, rows), out_shape=j...  59.9 us
    unnamed x1, local copies, waits for them, and re-layouts  3.27 us

profile of v1, /device:TPU:0, one launch (start us, length us, event | category | flops | bytes accessed | tf_op | source)
XLA Modules:
  0.0 63.2 jit_solution(5858293565781085987)
XLA Ops:
  0.0 59.9 %shard_map.109 = bf16[32,160,128]{2,1,0:T(8,128)(2,1)} custom-call(bf16[32,160,128]{2,1,0:T(8,128)(2,1)} %bitcast.5, s32[160,128]{1,0:T(8,128)} %bitcast.7, s32[4,32]{1,0:T(4,128)} %tile_id.1, f32[16,80]{1,0:T(8,128)} %tile_scale.1, bf16[128,128]{1,0:T(8,128)(2,1)} %inv_x.1, bf16[16,16]{1,0:T(8,128)(2,1)} %inv_y.1, bf16[80,80]{1,0:T(8,128)(2,1)} %inv_z.1, ...), custom_call_target="tpu_custom_call" | custom-call | tf_op jit(solution)/shard_map/pallas_call | solution.py:375
  59.9 3.3 %copy.13 = bf16[32,80,2,128]{3,2,1,0:T(2,128)(2,1)} copy(bf16[32,80,2,128]{3,2,1,0:T(2,128)(2,1)} %bitcast.4) | data formatting | bytes 2621440

commit v2 on v1

--- a/solution.py
+++ b/solution.py
@@ -33,18 +33,20 @@
     slots,
     tiles,
     rows,
-    control,
+    control_hbm,
     land,
     tile_id,
     tile_scale,
     inv_x,
     inv_y,
     inv_z,
-    pert,
+    pert_hbm,
     cells,
     values,
     weights,
     out,
+    control,
+    pert,
     sea,
     weight,
     ky,
@@ -74,8 +76,9 @@
     gather_rs,
     red_ss,
     red_rs,
+    load_sem,
 ):
-    members, depth, cols = control.shape
+    members, depth, cols = control_hbm.shape
     own = members // slots
     blocks = cols // LANES
     levels = depth // rows
@@ -92,6 +95,13 @@
         )
     for peer in (sib, far):
         pl.semaphore_signal(barrier, inc=1, device_id={"slot": peer}, device_id_type=MESH)
+
+    load_control = pltpu.make_async_copy(
+        control_hbm.at[pl.ds(s * own, own)], control, load_sem.at[0]
+    )
+    load_pert = pltpu.make_async_copy(pert_hbm, pert, load_sem.at[1])
+    load_control.start()
+    load_pert.start()
 
     region = tile_id[pl.ds(h * rows // 4, 1), :].astype(F32).astype(BF16)
     blocks_x = tile_id.shape[1]
@@ -138,19 +148,22 @@
             device_id_type=MESH,
         )
 
-    order = list(range(1, tiles)) + [0]
+    order = sorted(range(1, tiles), key=lambda d: abs(2 * d - tiles)) + [0]
+    place = {d: n for n, d in enumerate(order)}
+    arrive = [0] + order[:-1]
 
     first = []
+    load_control.wait()
     for d in order:
         u = lax.rem(h + d, tiles)
         k, c = u // blocks, lax.rem(u, blocks)
-        masked = (weight[...] * control[s * own + k].astype(F32)).astype(BF16)
+        masked = (weight[...] * control[k].astype(F32)).astype(BF16)
         along = (at_block(sea, c) * dot(masked, at_block(inv_x, c))).astype(BF16)
         if d == 0:
             recv_a[h] = along
         else:
             send_a[u] = along
-            if d == 1:
+            if d == order[0]:
                 pl.semaphore_wait(barrier, tiles - 1 + 2)
             copy = to_tile(0, d, send_a.at[u], recv_a.at[h])
             copy.start()
@@ -179,21 +192,6 @@
                 dot(matrix[...], part).astype(BF16).reshape(tiles, GROUP, LANES)
             )
 
-    for copy in first:
-        copy.wait_recv()
-    filter_y(ky_t, recv_a, across)
-    second = []
-    for d in order:
-        u = lax.rem(h + d, tiles)
-        deeper = dot(kz_t[...], across[u]).astype(BF16)
-        if d == 0:
-            spread[s * tiles + h] = deeper
-        else:
-            send_b[u] = deeper
-            copy = to_tile(1, d, send_b.at[u], spread.at[s * tiles + h])
-            copy.start()
-            second.append(copy)
-
     count = cells.shape[1]
     step = min(1024, count)
     shift = cols.bit_length() - 1
@@ -214,7 +212,24 @@
             obs_acc[n // 2] += dot(on_row, part, 1, 1)
         return carry
 
-    lax.fori_loop(0, count // step, observe, 0)
+    chunks = count // step
+    lax.fori_loop(0, chunks // 2, observe, 0)
+
+    for copy in first:
+        copy.wait_recv()
+    filter_y(ky_t, recv_a, across)
+    second = []
+    for d in order:
+        u = lax.rem(h + d, tiles)
+        deeper = dot(kz_t[...], across[u]).astype(BF16)
+        if d == 0:
+            spread[s * tiles + h] = deeper
+        else:
+            send_b[u] = deeper
+            copy = to_tile(1, d, send_b.at[u], spread.at[s * tiles + h])
+            copy.start()
+            second.append(copy)
+
 
     inc[...] = jnp.zeros_like(inc)
 
@@ -235,27 +250,28 @@
     def gather_copy(phase, d, unit, peer, buf):
         return to_slot(gather_ss, gather_rs, phase, d, buf.at[unit], buf.at[unit], peer)
 
-    arrive = [0] + list(range(1, tiles))
     core1, far1, fwd1 = [], [], []
-    for d in arrive:
+    load_pert.wait()
+    for n, d in enumerate(arrive):
         if d > 0:
-            second[d - 1].wait_recv()
+            second[place[d]].wait_recv()
         unit = s * tiles + source(d)
-        far1.append(gather_copy(1, d, unit, far, spread))
+        far1.append(gather_copy(1, n, unit, far, spread))
         far1[-1].start()
-        core1.append(gather_copy(0, d, unit, sib, spread))
+        core1.append(gather_copy(0, n, unit, sib, spread))
         core1[-1].start()
         add_member(s, source(d))
-    for d in arrive:
-        far1[d].wait_recv()
-        fwd1.append(gather_copy(2, d, far * tiles + source(d), sib, spread))
+    lax.fori_loop(chunks // 2, chunks, observe, 0)
+    for n, d in enumerate(arrive):
+        far1[n].wait_recv()
+        fwd1.append(gather_copy(2, n, far * tiles + source(d), sib, spread))
         fwd1[-1].start()
         add_member(far, source(d))
-    for d in arrive:
-        core1[d].wait_recv()
+    for n, d in enumerate(arrive):
+        core1[n].wait_recv()
         add_member(sib, source(d))
-    for d in arrive:
-        fwd1[d].wait_recv()
+    for n, d in enumerate(arrive):
+        fwd1[n].wait_recv()
         add_member(diag, source(d))
 
     norm = 1.0 / math.sqrt(members)
@@ -300,7 +316,7 @@
 
     for d in arrive:
         if d > 0:
-            third[d - 1].wait_recv()
+            third[place[d]].wait_recv()
         deep[source(d)] = dot(kz[...], recv_d[source(d)]).astype(BF16)
     filter_y(ky, deep, stage_e)
     fourth = []
@@ -321,7 +337,7 @@
         if blocks == 1:
             if n > 0:
                 fourth[n - 1].wait_recv()
-            k = source(n)
+            k = source(arrive[n])
             field = recv_e[k]
         else:
             k = n
@@ -329,14 +345,14 @@
         field = (field.astype(F32) * sea[...]).astype(BF16)
         m = s * own + k
         out[m] = (
-            control[m].astype(F32) + weight[...] * dot(field, inv_x[...], 1, 1)
+            control[k].astype(F32) + weight[...] * dot(field, inv_x[...], 1, 1)
         ).astype(BF16)
         far3.append(gather_copy(4, n, m, far, out))
         far3[-1].start()
         core3.append(gather_copy(3, n, m, sib, out))
         core3[-1].start()
     for n in range(own):
-        k = source(n) if blocks == 1 else n
+        k = source(arrive[n]) if blocks == 1 else n
         far3[n].wait_recv()
         fwd3.append(gather_copy(5, n, far * own + k, sib, out))
         fwd3[-1].start()
@@ -348,6 +364,12 @@
         + far3 + fwd3
     ):
         copy.wait_send()
+
+
+def store_kernel(src, dst, sem):
+    copy = pltpu.make_async_copy(src, dst, sem)
+    copy.start()
+    copy.wait()
 
 
 def per_device(
@@ -371,13 +393,16 @@
     assert slots == 4 and cols % LANES == 0 and cols & (cols - 1) == 0
     assert members // slots * blocks == tiles and depth % GROUP == 0 and 4 % rows == 0
     unit = (depth, LANES)
+    whole = pl.BlockSpec(memory_space=pl.ANY)
     vmem = pl.BlockSpec(memory_space=pltpu.VMEM)
     gradient = pl.pallas_call(
         functools.partial(kernel, slots, tiles, rows),
         out_shape=jax.ShapeDtypeStruct((members, depth, cols), BF16),
-        in_specs=[vmem] * 11,
+        in_specs=[whole] + [vmem] * 6 + [whole] + [vmem] * 3,
         out_specs=vmem,
         scratch_shapes=[
+            pltpu.VMEM((members // slots, depth, cols), BF16),
+            pltpu.VMEM((members, depth, cols), BF16),
             pltpu.VMEM((depth, cols), F32),
             pltpu.VMEM((depth, cols), F32),
             pltpu.VMEM((tiles * GROUP, tiles * GROUP), BF16),
@@ -407,6 +432,7 @@
             pltpu.SemaphoreType.DMA((6, tiles)),
             pltpu.SemaphoreType.DMA((3, tiles)),
             pltpu.SemaphoreType.DMA((3, tiles)),
+            pltpu.SemaphoreType.DMA((2,)),
         ],
         compiler_params=pltpu.CompilerParams(
             collective_id=0, has_side_effects=True, vmem_limit_bytes=56 * 1024 * 1024
@@ -424,6 +450,13 @@
         obs_value,
         obs_weight,
     )
+    gradient = pl.pallas_call(
+        store_kernel,
+        out_shape=jax.ShapeDtypeStruct(gradient.shape, BF16),
+        in_specs=[whole],
+        out_specs=whole,
+        scratch_shapes=[pltpu.SemaphoreType.DMA],
+    )(gradient)
     return gradient.reshape(members, levels, rows, cols)
 
 

time: 63.4 us -> 101 us (1.59)
  Pallas kernels: 59.9 us -> 101 us
  local copies, waits for them, and re-layouts: 3.27 us -> 0 us
    pallas_call x0 -> x1, Pallas kernels: none -> 40.8 us  [per_device(): pl.pallas_call(store_kernel, out_shape=jax.ShapeDtypeStruct(gradient.shap...]
    unnamed x1 -> x0, local copies, waits for them, and re-layouts: 3.27 us -> none
where the time goes in v2:
time: 101 us
  Pallas kernels  101 us (100%)
    pallas_call x1, Pallas kernels, per_device(): pl.pallas_call(functools.partial(kernel, slots, tiles, rows), out_shape=j...  59.9 us
    pallas_call x1, Pallas kernels, per_device(): pl.pallas_call(store_kernel, out_shape=jax.ShapeDtypeStruct(gradient.shap...  40.8 us

profile of v2, /device:TPU:0, one launch (start us, length us, event | category | flops | bytes accessed | tf_op | source)
XLA Modules:
  0.0 100.7 jit_solution(3071183165196260199)
XLA Ops:
  0.0 59.9 %shard_map.109.src = bf16[32,160,128]{2,1,0:T(8,128)(2,1)} custom-call(bf16[32,160,128]{2,1,0:T(8,128)(2,1)} %bitcast.4, s32[160,128]{1,0:T(8,128)} %bitcast.6, s32[4,32]{1,0:T(4,128)} %tile_id.1, f32[16,80]{1,0:T(8,128)} %tile_scale.1, bf16[128,128]{1,0:T(8,128)(2,1)} %inv_x.1, bf16[16,16]{1,0:T(8,128)(2,1)} %inv_y.1, bf16[80,80]{1,0:T(8,128)(2,1)} %inv_z.1, ...), custom_call_target="tpu_custom_call" | custom-call | tf_op jit(solution)/shard_map/pallas_call | solution.py:398
  59.9 40.8 %shard_map.110 = bf16[32,160,128]{2,1,0:T(8,128)(2,1)} custom-call(bf16[32,160,128]{2,1,0:T(8,128)(2,1)} %shard_map.109.src), custom_call_target="tpu_custom_call" | custom-call | tf_op jit(solution)/shard_map/pallas_call | solution.py:453

commit v3 on v2

v3 whole, which is shorter than its diff:
```python
import functools
import math

import jax
import jax.numpy as jnp
from jax import lax
from jax.experimental import pallas as pl
from jax.experimental.pallas import tpu as pltpu
from jax.sharding import PartitionSpec as P

LANES = 128
GROUP = 16
F32 = jnp.float32
BF16 = jnp.bfloat16
MESH = pl.DeviceIdType.MESH


def dot(a, b, ca=1, cb=0, precision=None):
    return lax.dot_general(
        a, b, (((ca,), (cb,)), ((), ())), preferred_element_type=F32, precision=precision
    )


def iota(shape, dim):
    return lax.broadcasted_iota(jnp.int32, shape, dim)


def spread_matrix(shape, index):
    return jnp.where(index == iota(shape, 1), 1.0, 0.0).astype(BF16)


def kernel(
    slots,
    tiles,
    rows,
    groups,
    control_hbm,
    land,
    tile_id,
    tile_scale,
    inv_x,
    inv_y,
    inv_z,
    pert_hbm,
    cells,
    values,
    weights,
    out,
    control,
    pert,
    sea,
    weight,
    ky,
    ky_t,
    kz,
    kz_t,
    obs_acc,
    inc,
    adj,
    send_a,
    recv_a,
    send_b,
    spread,
    stage_c,
    recv_c,
    stage_x,
    recv_x,
    stage_d,
    recv_d,
    deep,
    stage_e,
    recv_e,
    tile_ss,
    tile_rs,
    slot_ss,
    slot_rs,
    last_ss,
    last_rs,
    load_sem,
):
    members, depth, cols = control_hbm.shape
    own = members // slots
    blocks = cols // LANES
    levels = depth // rows
    part = depth // groups
    s = lax.axis_index("slot")
    h = lax.axis_index("horiz")
    sib = s + 1 - 2 * lax.rem(s, 2)
    far = s + 2 - 4 * (s // 2)
    diag = sib + 2 - 4 * (sib // 2)

    barrier = pltpu.get_barrier_semaphore()
    for d in range(1, tiles):
        pl.semaphore_signal(
            barrier, inc=1, device_id={"horiz": lax.rem(h + d, tiles)}, device_id_type=MESH
        )
    for peer in (sib, far):
        pl.semaphore_signal(barrier, inc=1, device_id={"slot": peer}, device_id_type=MESH)

    load_control = pltpu.make_async_copy(
        control_hbm.at[pl.ds(s * own, own)], control, load_sem.at[0]
    )
    load_pert = pltpu.make_async_copy(pert_hbm, pert, load_sem.at[1])
    load_control.start()
    load_pert.start()

    def target(n):
        return lax.rem(h + 1 + n, tiles)

    def source(n):
        return lax.rem(h - 1 - n + 2 * tiles, tiles)

    def each(count, body):
        if count <= 8:
            for n in range(count):
                body(n)
        else:
            lax.fori_loop(0, count, lambda n, carry: (body(n), carry)[1], 0)

    def at_block(ref, c, where=slice(None)):
        if blocks == 1:
            return ref[where]
        return ref[where, pl.ds(pl.multiple_of(c * LANES, LANES), LANES)]

    def pert_rows(slot, unit, where):
        k, c = unit // blocks, lax.rem(unit, blocks)
        if blocks == 1:
            return pert[slot * own + k, where].astype(F32)
        lanes = pl.ds(pl.multiple_of(c * LANES, LANES), LANES)
        return pert[slot * own + k, where, lanes].astype(F32)

    def rows_of(g):
        return slice(g * part, (g + 1) * part)

    def to_tile(phase, g, n, src, dst):
        return pltpu.make_async_remote_copy(
            src_ref=src,
            dst_ref=dst,
            send_sem=tile_ss.at[phase, g, n],
            recv_sem=tile_rs.at[phase, g, n],
            device_id={"horiz": target(n)},
            device_id_type=MESH,
        )

    def to_slot(phase, g, src, dst, peer):
        return pltpu.make_async_remote_copy(
            src_ref=src,
            dst_ref=dst,
            send_sem=slot_ss.at[phase, g],
            recv_sem=slot_rs.at[phase, g],
            device_id={"slot": peer},
            device_id_type=MESH,
        )

    def copy_a(g, n):
        return to_tile(0, g, n, send_a.at[g, n], recv_a.at[g, h])

    def copy_b(g, n):
        return to_tile(1, g, n, send_b.at[g, target(n)], spread.at[g, s, n])

    def copy_d(g, n):
        return to_tile(2, g, n, stage_d.at[g, n], recv_d.at[g, h])

    def copy_e(n):
        return to_tile(3, 0, n, stage_e.at[target(n)], recv_e.at[n])

    def copy_far(g):
        return to_slot(0, g, spread.at[g, s], spread.at[g, s], far)

    def copy_core(g):
        return to_slot(1, g, spread.at[g, s], spread.at[g, s], sib)

    def copy_on(g):
        return to_slot(2, g, spread.at[g, far], spread.at[g, far], sib)

    def copy_sum(g, n):
        return to_slot(3 + n, g, stage_c.at[g, n], recv_c.at[g, n], sib)

    def copy_x(g):
        return to_slot(5, g, stage_x.at[g], recv_x.at[g], far)

    def copy_last(phase, n, m, peer):
        return pltpu.make_async_remote_copy(
            src_ref=out.at[m],
            dst_ref=out.at[m],
            send_sem=last_ss.at[phase, n],
            recv_sem=last_rs.at[phase, n],
            device_id={"slot": peer},
            device_id_type=MESH,
        )

    others = tiles - 1

    region = tile_id[pl.ds(h * rows // 4, 1), :].astype(F32).astype(BF16)
    blocks_x = tile_id.shape[1]
    widen = jnp.where(iota((blocks_x, cols), 1) // 4 == iota((blocks_x, cols), 0), 1.0, 0.0)
    region_x = dot(region, widen.astype(BF16))
    regions = tile_scale.shape[0]
    onehot = jnp.where(iota((regions, cols), 0).astype(F32) == region_x, 1.0, 0.0)
    to_level = spread_matrix((depth, levels), iota((depth, levels), 0) // rows)
    scale_rows = dot(
        to_level.astype(F32), tile_scale[...], 1, 1, precision=lax.Precision.HIGHEST
    )
    sea[...] = land[...].astype(F32)
    weight[...] = sea[...] * dot(scale_rows, onehot, precision=lax.Precision.HIGHEST)

    same = lax.rem(iota((depth, depth), 0), rows) == lax.rem(iota((depth, depth), 1), rows)
    half = dot(to_level, inv_z[...], 1, 1).astype(BF16)
    kz_t[...] = jnp.where(same, dot(half, to_level, 1, 1), 0.0).astype(BF16)

    load_control.wait()

    def forward(n):
        u = target(n)
        k, c = u // blocks, lax.rem(u, blocks)
        masked = (weight[...] * control[k].astype(F32)).astype(BF16)
        along = (at_block(sea, c) * dot(masked, at_block(inv_x, c))).astype(BF16)
        return dot(kz_t[...], along).astype(BF16).reshape(groups, part, LANES)

    pl.semaphore_wait(barrier, tiles - 1 + 2)

    def send_first(n):
        send_a[:, n] = forward(n)
        copy_a(0, n).start()

    each(others, send_first)
    for g in range(1, groups):
        each(others, lambda n: copy_a(g, n).start())
    mine = forward(others)
    for g in range(groups):
        recv_a[g, h] = mine[g]

    wide = tiles * GROUP
    side = tiles * rows
    pos = iota((wide, side), 0)
    pick_y = spread_matrix((wide, side), pos // GROUP * rows + lax.rem(pos, rows))
    row_i, col_i = iota((wide, wide), 0), iota((wide, wide), 1)
    same_level = lax.rem(row_i, GROUP) // rows == lax.rem(col_i, GROUP) // rows
    half = dot(pick_y, inv_y[...], 1, 1).astype(BF16)
    ky_t[...] = jnp.where(same_level, dot(half, pick_y, 1, 1), 0.0).astype(BF16)

    def filter_y(matrix, src, dst, g):
        for i in range(part // GROUP):
            some = src[g, :, i * GROUP : (i + 1) * GROUP, :].reshape(wide, LANES)
            dst[g, :, i * GROUP : (i + 1) * GROUP, :] = (
                dot(matrix[...], some).astype(BF16).reshape(tiles, GROUP, LANES)
            )

    count = cells.shape[1]
    step = min(1024, count)
    chunks = count // step
    shift = cols.bit_length() - 1
    obs_acc[...] = jnp.zeros_like(obs_acc)

    def observe(i, carry):
        where = pl.ds(pl.multiple_of(i * step, step), step)
        cell, w = cells[:, where], weights[:, where]
        wv = w * values[:, where]
        w_hi = w.astype(BF16).astype(F32)
        v_hi = wv.astype(BF16).astype(F32)
        on_row = jnp.where(iota((depth, step), 0) == (cell >> shift), 1.0, 0.0).astype(BF16)
        on_col = iota((cols, step), 0) == (cell & (cols - 1))
        parts = [
            jnp.where(on_col, x, 0.0).astype(BF16) for x in (w_hi, w - w_hi, v_hi, wv - v_hi)
        ]
        for n, x in enumerate(parts):
            obs_acc[n // 2] += dot(on_row, x, 1, 1)
        return carry

    ahead = max(chunks - groups, 0)
    lax.fori_loop(0, ahead, observe, 0)
    inc[...] = jnp.zeros_like(inc)

    for g in range(groups):
        each(others, lambda n: copy_a(g, n).wait_recv())
        filter_y(ky_t, recv_a, send_b, g)
        each(others, lambda n: copy_b(g, n).start())
        spread[g, s, others] = send_b[g, h]
        begin = min(ahead + g, chunks)
        lax.fori_loop(begin, chunks if g == groups - 1 else min(begin + 1, chunks), observe, 0)
    load_pert.wait()

    norm = 1.0 / math.sqrt(members)

    def add_slot(g, slot):
        where = rows_of(g)

        def one(n):
            unit = source(n)
            term = pert_rows(slot, unit, where) * spread[g, slot, n].astype(F32)
            if blocks == 1:
                inc[where] += term
            else:
                c = lax.rem(unit, blocks)
                inc[where, pl.ds(pl.multiple_of(c * LANES, LANES), LANES)] += term

        each(tiles, one)

    def partial(g, slot, n):
        u = target(n)
        return pert_rows(slot, u, rows_of(g)) * at_block(adj, lax.rem(u, blocks), rows_of(g))

    def gather(g):
        each(others, lambda n: copy_b(g, n).wait_recv())
        copy_far(g).start()
        copy_core(g).start()
        add_slot(g, s)

    def pass_on(g):
        copy_far(g).wait_recv()
        copy_on(g).start()
        add_slot(g, far)
        copy_core(g).wait_recv()
        add_slot(g, sib)

    def observed(g):
        copy_on(g).wait_recv()
        add_slot(g, diag)
        where = rows_of(g)
        adj[where] = sea[where] * (
            (inc[where] * norm * obs_acc[0, where] - obs_acc[1, where]) * norm
        )
        for i, slot in enumerate((diag, sib)):

            def fill(n):
                stage_c[g, i, n] = partial(g, slot, n).astype(BF16)

            each(tiles, fill)
            copy_sum(g, i).start()

    def between_chips(g):
        copy_sum(g, 0).wait_recv()

        def fill(n):
            stage_x[g, n] = (partial(g, far, n) + recv_c[g, 0, n].astype(F32)).astype(BF16)

        each(tiles, fill)
        copy_x(g).start()

    def exchange(g):
        copy_sum(g, 1).wait_recv()
        copy_x(g).wait_recv()

        def total(n):
            value = partial(g, s, n) + recv_c[g, 1, n].astype(F32) + recv_x[g, n].astype(F32)
            return value.astype(BF16)

        def fill(n):
            stage_d[g, n] = total(n)
            copy_d(g, n).start()

        each(others, fill)
        recv_d[g, h] = total(others)

    stages = ((0, gather), (2, pass_on), (3, observed), (4, between_chips), (5, exchange))
    for t in range(groups + 5):
        for delay, stage in stages:
            if 0 <= t - delay < groups:
                stage(t - delay)
        if t == groups:
            half = dot(pick_y, inv_y[...]).astype(BF16)
            ky[...] = jnp.where(same_level, dot(half, pick_y, 1, 1), 0.0).astype(BF16)
            half = dot(to_level, inv_z[...]).astype(BF16)
            kz[...] = jnp.where(same, dot(half, to_level, 1, 1), 0.0).astype(BF16)

    for g in range(groups):
        each(others, lambda n: copy_a(g, n).wait_send())
        each(others, lambda n: copy_b(g, n).wait_send())
        for copy in (copy_far, copy_core, copy_on):
            copy(g).wait_send()
    for g in range(groups):
        each(others, lambda n: copy_d(g, n).wait_recv())
        filter_y(ky, recv_d, deep, g)

    def adjoint(u):
        return dot(kz[...], deep[:, u].reshape(depth, LANES)).astype(BF16)

    def send_last(n):
        stage_e[target(n)] = adjoint(target(n))
        copy_e(n).start()

    each(others, send_last)
    recv_e[others] = adjoint(h)

    def member(n):
        if blocks > 1:
            return n
        return source(n)

    if blocks > 1:
        each(others, lambda n: copy_e(n).wait_recv())
    turns = [own - 1] + list(range(own - 1))
    for n in turns:
        k = member(n)
        if blocks == 1:
            if n < others:
                copy_e(n).wait_recv()
            field = recv_e[n]
        else:
            field = jnp.concatenate(
                [recv_e[source(n * blocks + c)] for c in range(blocks)], axis=1
            )
        field = (field.astype(F32) * sea[...]).astype(BF16)
        m = s * own + k
        out[m] = (
            control[k].astype(F32) + weight[...] * dot(field, inv_x[...], 1, 1)
        ).astype(BF16)
        copy_last(0, n, m, far).start()
        copy_last(1, n, m, sib).start()
    for n in turns:
        copy_last(0, n, s * own + member(n), far).wait_recv()
        copy_last(2, n, far * own + member(n), sib).start()
    for g in range(groups):
        each(others, lambda n: copy_d(g, n).wait_send())
        copy_sum(g, 0).wait_send()
        copy_sum(g, 1).wait_send()
        copy_x(g).wait_send()
    each(others, lambda n: copy_e(n).wait_send())
    for n in turns:
        for phase, slot, peer in ((0, s, far), (1, s, sib), (2, far, sib)):
            copy = copy_last(phase, n, slot * own + member(n), peer)
            copy.wait_send()
            if phase > 0:
                copy.wait_recv()


def store_kernel(src, dst):
    dst[...] = src[...]


def per_device(
    slots,
    tiles,
    control,
    land_mask,
    tile_id,
    tile_scale,
    inverse_x,
    inverse_y,
    inverse_z,
    perturbations,
    obs_cell,
    obs_value,
    obs_weight,
):
    members, levels, rows, cols = control.shape
    depth = levels * rows
    blocks = cols // LANES
    assert slots == 4 and cols % LANES == 0 and cols & (cols - 1) == 0
    assert members // slots * blocks == tiles and depth % GROUP == 0 and 4 % rows == 0
    groups = next(n for n in (5, 2, 1) if depth % (n * GROUP) == 0)
    piece = (depth // groups, LANES)
    units = (groups, tiles) + piece
    whole = pl.BlockSpec(memory_space=pl.ANY)
    vmem = pl.BlockSpec(memory_space=pltpu.VMEM)
    gradient = pl.pallas_call(
        functools.partial(kernel, slots, tiles, rows, groups),
        out_shape=jax.ShapeDtypeStruct((members, depth, cols), BF16),
        in_specs=[whole] + [vmem] * 6 + [whole] + [vmem] * 3,
        out_specs=vmem,
        scratch_shapes=[
            pltpu.VMEM((members // slots, depth, cols), BF16),
            pltpu.VMEM((members, depth, cols), BF16),
            pltpu.VMEM((depth, cols), F32),
            pltpu.VMEM((depth, cols), F32),
            pltpu.VMEM((tiles * GROUP, tiles * GROUP), BF16),
            pltpu.VMEM((tiles * GROUP, tiles * GROUP), BF16),
            pltpu.VMEM((depth, depth), BF16),
            pltpu.VMEM((depth, depth), BF16),
            pltpu.VMEM((2, depth, cols), F32),
            pltpu.VMEM((depth, cols), F32),
            pltpu.VMEM((depth, cols), F32),
            pltpu.VMEM(units, BF16),
            pltpu.VMEM(units, BF16),
            pltpu.VMEM(units, BF16),
            pltpu.VMEM((groups, slots, tiles) + piece, BF16),
            pltpu.VMEM((groups, 2, tiles) + piece, BF16),
            pltpu.VMEM((groups, 2, tiles) + piece, BF16),
            pltpu.VMEM(units, BF16),
            pltpu.VMEM(units, BF16),
            pltpu.VMEM(units, BF16),
            pltpu.VMEM(units, BF16),
            pltpu.VMEM(units, BF16),
            pltpu.VMEM((tiles, depth, LANES), BF16),
            pltpu.VMEM((tiles, depth, LANES), BF16),
            pltpu.SemaphoreType.DMA((4, groups, tiles)),
            pltpu.SemaphoreType.DMA((4, groups, tiles)),
            pltpu.SemaphoreType.DMA((6, groups)),
            pltpu.SemaphoreType.DMA((6, groups)),
            pltpu.SemaphoreType.DMA((3, members // slots)),
            pltpu.SemaphoreType.DMA((3, members // slots)),
            pltpu.SemaphoreType.DMA((2,)),
        ],
        compiler_params=pltpu.CompilerParams(
            collective_id=0, has_side_effects=True, vmem_limit_bytes=56 * 1024 * 1024
        ),
    )(
        control.reshape(members, depth, cols),
        land_mask.reshape(depth, cols),
        tile_id,
        tile_scale,
        inverse_x,
        inverse_y,
        inverse_z,
        perturbations.reshape(members, depth, cols),
        obs_cell,
        obs_value,
        obs_weight,
    )
    block = pl.BlockSpec((members // 4, depth, cols), lambda i: (i, 0, 0))
    gradient = pl.pallas_call(
        store_kernel,
        out_shape=jax.ShapeDtypeStruct(gradient.shape, BF16),
        grid=(4,),
        in_specs=[block],
        out_specs=block,
    )(gradient)
    return gradient.reshape(members, levels, rows, cols)


def solution(mesh):
    return jax.shard_map(
        functools.partial(per_device, mesh.shape["slot"], mesh.shape["horiz"]),
        mesh=mesh,
        in_specs=(
            P(None, None, "horiz", None),
            P(None, "horiz", None),
            P(),
            P(),
            P(),
            P(),
            P(),
            P("slot", None, None, "horiz", None),
            P("slot", "horiz"),
            P("slot", "horiz"),
            P("slot", "horiz"),
        ),
        out_specs=P(None, None, "horiz", None),
        check_vma=False,
    )
```

time: 101 us -> 63.9 us (0.63)
  Pallas kernels: 101 us -> 63.6 us
    pallas_call x1, Pallas kernels: 40.8 us -> 3.47 us  [per_device(): pl.pallas_call(store_kernel, out_shape=jax.ShapeDtypeStruct(gradient.shap...]
where the time goes in v3:
time: 63.9 us; the launch traced here: 63.6 us
  Pallas kernels  63.6 us (100%)
    pallas_call x1, Pallas kernels, per_device(): pl.pallas_call(functools.partial(kernel, slots, tiles, rows, groups), out...  60.2 us
    pallas_call x1, Pallas kernels, per_device(): pl.pallas_call(store_kernel, out_shape=jax.ShapeDtypeStruct(gradient.shap...  3.47 us

profile of v3, /device:TPU:0, one launch (start us, length us, event | category | flops | bytes accessed | tf_op | source)
XLA Modules:
  0.0 63.6 jit_solution(4581451225055626254)
XLA Ops:
  0.0 60.2 %shard_map.109.src = bf16[32,160,128]{2,1,0:T(8,128)(2,1)} custom-call(bf16[32,160,128]{2,1,0:T(8,128)(2,1)} %bitcast.4, s32[160,128]{1,0:T(8,128)} %bitcast.6, s32[4,32]{1,0:T(4,128)} %tile_id.1, f32[16,80]{1,0:T(8,128)} %tile_scale.1, bf16[128,128]{1,0:T(8,128)(2,1)} %inv_x.1, bf16[16,16]{1,0:T(8,128)(2,1)} %inv_y.1, bf16[80,80]{1,0:T(8,128)(2,1)} %inv_z.1, ...), custom_call_target="tpu_custom_call" | custom-call | tf_op jit(solution)/shard_map/pallas_call | solution.py:456
  60.2 3.5 %shard_map.110 = bf16[32,160,128]{2,1,0:T(8,128)(2,1)} custom-call(bf16[32,160,128]{2,1,0:T(8,128)(2,1)} %shard_map.109.src), custom_call_target="tpu_custom_call" | custom-call | tf_op jit(solution)/shard_map/pallas_call | solution.py:511

commit v4 on v3

--- a/solution.py
+++ b/solution.py
@@ -55,6 +55,7 @@
     kz,
     kz_t,
     obs_acc,
+    cell_sum,
     inc,
     adj,
     send_a,
@@ -263,11 +264,10 @@
         parts = [
             jnp.where(on_col, x, 0.0).astype(BF16) for x in (w_hi, w - w_hi, v_hi, wv - v_hi)
         ]
-        for n, x in enumerate(parts):
-            obs_acc[n // 2] += dot(on_row, x, 1, 1)
+        obs_acc[...] += dot(jnp.concatenate(parts, axis=0), on_row, 1, 1)
         return carry
 
-    ahead = max(chunks - groups, 0)
+    ahead = chunks // 2
     lax.fori_loop(0, ahead, observe, 0)
     inc[...] = jnp.zeros_like(inc)
 
@@ -276,8 +276,11 @@
         filter_y(ky_t, recv_a, send_b, g)
         each(others, lambda n: copy_b(g, n).start())
         spread[g, s, others] = send_b[g, h]
-        begin = min(ahead + g, chunks)
-        lax.fori_loop(begin, chunks if g == groups - 1 else min(begin + 1, chunks), observe, 0)
+    lax.fori_loop(ahead, chunks, observe, 0)
+    for i in range(2):
+        both = obs_acc[2 * i * cols : (2 * i + 1) * cols]
+        both += obs_acc[(2 * i + 1) * cols : (2 * i + 2) * cols]
+        cell_sum[i] = both.T
     load_pert.wait()
 
     norm = 1.0 / math.sqrt(members)
@@ -318,7 +321,7 @@
         add_slot(g, diag)
         where = rows_of(g)
         adj[where] = sea[where] * (
-            (inc[where] * norm * obs_acc[0, where] - obs_acc[1, where]) * norm
+            (inc[where] * norm * cell_sum[0, where] - cell_sum[1, where]) * norm
         )
         for i, slot in enumerate((diag, sib)):
 
@@ -424,8 +427,20 @@
                 copy.wait_recv()
 
 
-def store_kernel(src, dst):
-    dst[...] = src[...]
+def store_kernel(src, dst, held, sems):
+    count = held.shape[0]
+    size = src.shape[0] // count
+    loads, stores = [], []
+    for i in range(count):
+        where = pl.ds(i * size, size)
+        loads.append(pltpu.make_async_copy(src.at[where], held.at[i], sems.at[0, i]))
+        stores.append(pltpu.make_async_copy(held.at[i], dst.at[where], sems.at[1, i]))
+        loads[-1].start()
+    for load, store in zip(loads, stores):
+        load.wait()
+        store.start()
+    for store in stores:
+        store.wait()
 
 
 def per_device(
@@ -448,7 +463,7 @@
     blocks = cols // LANES
     assert slots == 4 and cols % LANES == 0 and cols & (cols - 1) == 0
     assert members // slots * blocks == tiles and depth % GROUP == 0 and 4 % rows == 0
-    groups = next(n for n in (5, 2, 1) if depth % (n * GROUP) == 0)
+    groups = next(n for n in (2, 1) if depth % (n * GROUP) == 0)
     piece = (depth // groups, LANES)
     units = (groups, tiles) + piece
     whole = pl.BlockSpec(memory_space=pl.ANY)
@@ -467,6 +482,7 @@
             pltpu.VMEM((tiles * GROUP, tiles * GROUP), BF16),
             pltpu.VMEM((depth, depth), BF16),
             pltpu.VMEM((depth, depth), BF16),
+            pltpu.VMEM((4 * cols, depth), F32),
             pltpu.VMEM((2, depth, cols), F32),
             pltpu.VMEM((depth, cols), F32),
             pltpu.VMEM((depth, cols), F32),
@@ -507,13 +523,16 @@
         obs_value,
         obs_weight,
     )
-    block = pl.BlockSpec((members // 4, depth, cols), lambda i: (i, 0, 0))
     gradient = pl.pallas_call(
         store_kernel,
         out_shape=jax.ShapeDtypeStruct(gradient.shape, BF16),
-        grid=(4,),
-        in_specs=[block],
-        out_specs=block,
+        in_specs=[whole],
+        out_specs=whole,
+        scratch_shapes=[
+            pltpu.VMEM((8, members // 8, depth, cols), BF16),
+            pltpu.SemaphoreType.DMA((2, 8)),
+        ],
+        compiler_params=pltpu.CompilerParams(vmem_limit_bytes=56 * 1024 * 1024),
     )(gradient)
     return gradient.reshape(members, levels, rows, cols)
 

time: 63.9 us -> 65 us (1.017)
  Pallas kernels: 63.6 us -> 64.8 us
    pallas_call x1, Pallas kernels: 60.2 us -> 62.6 us  [per_device(): pl.pallas_call(functools.partial(kernel, slots, tiles, rows, groups), out...]
    pallas_call x1, Pallas kernels: 3.47 us -> 2.21 us  [per_device(): pl.pallas_call(store_kernel, out_shape=jax.ShapeDtypeStruct(gradient.shap...]
where the time goes in v4:
time: 65 us; the launch traced here: 64.8 us
  Pallas kernels  64.8 us (100%)
    pallas_call x1, Pallas kernels, per_device(): pl.pallas_call(functools.partial(kernel, slots, tiles, rows, groups), out...  62.6 us
    pallas_call x1, Pallas kernels, per_device(): pl.pallas_call(store_kernel, out_shape=jax.ShapeDtypeStruct(gradient.shap...  2.21 us

profile of v4, /device:TPU:0, one launch (start us, length us, event | category | flops | bytes accessed | tf_op | source)
XLA Modules:
  0.0 64.8 jit_solution(10696762655707409872)
XLA Ops:
  0.0 62.6 %shard_map.109.src = bf16[32,160,128]{2,1,0:T(8,128)(2,1)} custom-call(bf16[32,160,128]{2,1,0:T(8,128)(2,1)} %bitcast.4, s32[160,128]{1,0:T(8,128)} %bitcast.6, s32[4,32]{1,0:T(4,128)} %tile_id.1, f32[16,80]{1,0:T(8,128)} %tile_scale.1, bf16[128,128]{1,0:T(8,128)(2,1)} %inv_x.1, bf16[16,16]{1,0:T(8,128)(2,1)} %inv_y.1, bf16[80,80]{1,0:T(8,128)(2,1)} %inv_z.1, ...), custom_call_target="tpu_custom_call" | custom-call | tf_op jit(solution)/shard_map/pallas_call | solution.py:471
  62.6 2.2 %shard_map.110 = bf16[32,160,128]{2,1,0:T(8,128)(2,1)} custom-call(bf16[32,160,128]{2,1,0:T(8,128)(2,1)} %shard_map.109.src), custom_call_target="tpu_custom_call" | custom-call | tf_op jit(solution)/shard_map/pallas_call | solution.py:526

commit v5 on v4

--- a/solution.py
+++ b/solution.py
@@ -105,11 +105,14 @@
     load_control.start()
     load_pert.start()
 
+    def distance(n):
+        return tiles // 2 + (1 - 2 * (n % 2)) * ((n + 1) // 2)
+
     def target(n):
-        return lax.rem(h + 1 + n, tiles)
+        return lax.rem(h + distance(n), tiles)
 
     def source(n):
-        return lax.rem(h - 1 - n + 2 * tiles, tiles)
+        return lax.rem(h - distance(n) + tiles, tiles)
 
     def each(count, body):
         if count <= 8:
@@ -143,12 +146,12 @@
             device_id_type=MESH,
         )
 
-    def to_slot(phase, g, src, dst, peer):
+    def to_slot(phase, g, n, src, dst, peer):
         return pltpu.make_async_remote_copy(
             src_ref=src,
             dst_ref=dst,
-            send_sem=slot_ss.at[phase, g],
-            recv_sem=slot_rs.at[phase, g],
+            send_sem=slot_ss.at[phase, g, n],
+            recv_sem=slot_rs.at[phase, g, n],
             device_id={"slot": peer},
             device_id_type=MESH,
         )
@@ -159,26 +162,26 @@
     def copy_b(g, n):
         return to_tile(1, g, n, send_b.at[g, target(n)], spread.at[g, s, n])
 
-    def copy_d(g, n):
-        return to_tile(2, g, n, stage_d.at[g, n], recv_d.at[g, h])
+    def copy_d(n):
+        return to_tile(2, 0, n, stage_d.at[n], recv_d.at[h])
 
     def copy_e(n):
-        return to_tile(3, 0, n, stage_e.at[target(n)], recv_e.at[n])
-
-    def copy_far(g):
-        return to_slot(0, g, spread.at[g, s], spread.at[g, s], far)
-
-    def copy_core(g):
-        return to_slot(1, g, spread.at[g, s], spread.at[g, s], sib)
-
-    def copy_on(g):
-        return to_slot(2, g, spread.at[g, far], spread.at[g, far], sib)
-
-    def copy_sum(g, n):
-        return to_slot(3 + n, g, stage_c.at[g, n], recv_c.at[g, n], sib)
-
-    def copy_x(g):
-        return to_slot(5, g, stage_x.at[g], recv_x.at[g], far)
+        return to_tile(3, 0, n, stage_e.at[target(n)], recv_e.at[h])
+
+    def copy_far(g, n):
+        return to_slot(0, g, n, spread.at[g, s, n], spread.at[g, s, n], far)
+
+    def copy_core(g, n):
+        return to_slot(1, g, n, spread.at[g, s, n], spread.at[g, s, n], sib)
+
+    def copy_on(g, n):
+        return to_slot(2, g, n, spread.at[g, far, n], spread.at[g, far, n], sib)
+
+    def copy_sum(i, n):
+        return to_slot(3 + i, 0, n, stage_c.at[i, n], recv_c.at[i, n], sib)
+
+    def copy_x(n):
+        return to_slot(5, 0, n, stage_x.at[n], recv_x.at[n], far)
 
     def copy_last(phase, n, m, peer):
         return pltpu.make_async_remote_copy(
@@ -285,105 +288,104 @@
 
     norm = 1.0 / math.sqrt(members)
 
-    def add_slot(g, slot):
+    def add_unit(g, slot, n):
         where = rows_of(g)
-
-        def one(n):
-            unit = source(n)
-            term = pert_rows(slot, unit, where) * spread[g, slot, n].astype(F32)
-            if blocks == 1:
-                inc[where] += term
-            else:
-                c = lax.rem(unit, blocks)
-                inc[where, pl.ds(pl.multiple_of(c * LANES, LANES), LANES)] += term
-
-        each(tiles, one)
-
-    def partial(g, slot, n):
+        unit = source(n)
+        term = pert_rows(slot, unit, where) * spread[g, slot, n].astype(F32)
+        if blocks == 1:
+            inc[where] += term
+        else:
+            c = lax.rem(unit, blocks)
+            inc[where, pl.ds(pl.multiple_of(c * LANES, LANES), LANES)] += term
+
+    def gather(g, n):
+        if not isinstance(n, int) or n < others:
+            copy_b(g, n).wait_recv()
+        copy_far(g, n).start()
+        copy_core(g, n).start()
+        add_unit(g, s, n)
+
+    def pass_on(g, n):
+        copy_far(g, n).wait_recv()
+        copy_on(g, n).start()
+        add_unit(g, far, n)
+        copy_core(g, n).wait_recv()
+        add_unit(g, sib, n)
+
+    def finish(g, n):
+        copy_on(g, n).wait_recv()
+        add_unit(g, diag, n)
+
+    for g in range(groups):
+        copy_far(g, others).start()
+        copy_core(g, others).start()
+        add_unit(g, s, others)
+        each(others, lambda n: gather(g, n))
+    half = dot(pick_y, inv_y[...]).astype(BF16)
+    ky[...] = jnp.where(same_level, dot(half, pick_y, 1, 1), 0.0).astype(BF16)
+    half = dot(to_level, inv_z[...]).astype(BF16)
+    kz[...] = jnp.where(same, dot(half, to_level, 1, 1), 0.0).astype(BF16)
+    for g in range(groups):
+        pass_on(g, others)
+        each(others, lambda n: pass_on(g, n))
+    for g in range(groups):
+        finish(g, others)
+        each(others, lambda n: finish(g, n))
+    adj[...] = sea[...] * ((inc[...] * norm * cell_sum[0] - cell_sum[1]) * norm)
+
+    def partial(slot, n):
         u = target(n)
-        return pert_rows(slot, u, rows_of(g)) * at_block(adj, lax.rem(u, blocks), rows_of(g))
-
-    def gather(g):
-        each(others, lambda n: copy_b(g, n).wait_recv())
-        copy_far(g).start()
-        copy_core(g).start()
-        add_slot(g, s)
-
-    def pass_on(g):
-        copy_far(g).wait_recv()
-        copy_on(g).start()
-        add_slot(g, far)
-        copy_core(g).wait_recv()
-        add_slot(g, sib)
-
-    def observed(g):
-        copy_on(g).wait_recv()
-        add_slot(g, diag)
-        where = rows_of(g)
-        adj[where] = sea[where] * (
-            (inc[where] * norm * cell_sum[0, where] - cell_sum[1, where]) * norm
-        )
-        for i, slot in enumerate((diag, sib)):
-
-            def fill(n):
-                stage_c[g, i, n] = partial(g, slot, n).astype(BF16)
-
-            each(tiles, fill)
-            copy_sum(g, i).start()
-
-    def between_chips(g):
-        copy_sum(g, 0).wait_recv()
-
-        def fill(n):
-            stage_x[g, n] = (partial(g, far, n) + recv_c[g, 0, n].astype(F32)).astype(BF16)
-
-        each(tiles, fill)
-        copy_x(g).start()
-
-    def exchange(g):
-        copy_sum(g, 1).wait_recv()
-        copy_x(g).wait_recv()
-
-        def total(n):
-            value = partial(g, s, n) + recv_c[g, 1, n].astype(F32) + recv_x[g, n].astype(F32)
-            return value.astype(BF16)
-
-        def fill(n):
-            stage_d[g, n] = total(n)
-            copy_d(g, n).start()
-
-        each(others, fill)
-        recv_d[g, h] = total(others)
-
-    stages = ((0, gather), (2, pass_on), (3, observed), (4, between_chips), (5, exchange))
-    for t in range(groups + 5):
-        for delay, stage in stages:
-            if 0 <= t - delay < groups:
-                stage(t - delay)
-        if t == groups:
-            half = dot(pick_y, inv_y[...]).astype(BF16)
-            ky[...] = jnp.where(same_level, dot(half, pick_y, 1, 1), 0.0).astype(BF16)
-            half = dot(to_level, inv_z[...]).astype(BF16)
-            kz[...] = jnp.where(same, dot(half, to_level, 1, 1), 0.0).astype(BF16)
+        return pert_rows(slot, u, slice(None)) * at_block(adj, lax.rem(u, blocks))
+
+    for i, slot in enumerate((diag, sib)):
+
+        def to_core(n):
+            stage_c[i, n] = partial(slot, n).astype(BF16)
+            copy_sum(i, n).start()
+
+        each(tiles, to_core)
+
+    def between_chips(n):
+        copy_sum(0, n).wait_recv()
+        stage_x[n] = (partial(far, n) + recv_c[0, n].astype(F32)).astype(BF16)
+        copy_x(n).start()
+
+    each(tiles, between_chips)
+
+    def total(n):
+        copy_sum(1, n).wait_recv()
+        copy_x(n).wait_recv()
+        value = partial(s, n) + recv_c[1, n].astype(F32) + recv_x[n].astype(F32)
+        return value.astype(BF16)
+
+    def exchange(n):
+        stage_d[n] = total(n)
+        copy_d(n).start()
+
+    each(others, exchange)
+    recv_d[h] = total(others)
 
     for g in range(groups):
         each(others, lambda n: copy_a(g, n).wait_send())
         each(others, lambda n: copy_b(g, n).wait_send())
         for copy in (copy_far, copy_core, copy_on):
-            copy(g).wait_send()
-    for g in range(groups):
-        each(others, lambda n: copy_d(g, n).wait_recv())
-        filter_y(ky, recv_d, deep, g)
-
-    def adjoint(u):
-        return dot(kz[...], deep[:, u].reshape(depth, LANES)).astype(BF16)
-
-    def send_last(n):
-        stage_e[target(n)] = adjoint(target(n))
-        copy_e(n).start()
-
-    each(others, send_last)
-    recv_e[others] = adjoint(h)
+            each(tiles, lambda n: copy(g, n).wait_send())
+
+    def adjoint_z(u):
+        deep[u] = dot(kz[...], recv_d[u]).astype(BF16)
+
+    def arrived(n):
+        copy_d(n).wait_recv()
+        adjoint_z(source(n))
+
+    adjoint_z(h)
+    each(others, arrived)
+    for i in range(depth // GROUP):
+        where = slice(i * GROUP, (i + 1) * GROUP)
+        some = deep[:, where, :].reshape(wide, LANES)
+        stage_e[:, where, :] = dot(ky[...], some).astype(BF16).reshape(tiles, GROUP, LANES)
+    each(others, lambda n: copy_e(n).start())
+    recv_e[h] = stage_e[h]
 
     def member(n):
         if blocks > 1:
@@ -398,10 +400,10 @@
         if blocks == 1:
             if n < others:
                 copy_e(n).wait_recv()
-            field = recv_e[n]
+            field = recv_e[k]
         else:
             field = jnp.concatenate(
-                [recv_e[source(n * blocks + c)] for c in range(blocks)], axis=1
+                [recv_e[n * blocks + c] for c in range(blocks)], axis=1
             )
         field = (field.astype(F32) * sea[...]).astype(BF16)
         m = s * own + k
@@ -413,12 +415,10 @@
     for n in turns:
         copy_last(0, n, s * own + member(n), far).wait_recv()
         copy_last(2, n, far * own + member(n), sib).start()
-    for g in range(groups):
-        each(others, lambda n: copy_d(g, n).wait_send())
-        copy_sum(g, 0).wait_send()
-        copy_sum(g, 1).wait_send()
-        copy_x(g).wait_send()
+    each(others, lambda n: copy_d(n).wait_send())
     each(others, lambda n: copy_e(n).wait_send())
+    for copy in (lambda n: copy_sum(0, n), lambda n: copy_sum(1, n), copy_x):
+        each(tiles, lambda n: copy(n).wait_send())
     for n in turns:
         for phase, slot, peer in ((0, s, far), (1, s, sib), (2, far, sib)):
             copy = copy_last(phase, n, slot * own + member(n), peer)
@@ -466,6 +466,7 @@
     groups = next(n for n in (2, 1) if depth % (n * GROUP) == 0)
     piece = (depth // groups, LANES)
     units = (groups, tiles) + piece
+    columns = (tiles, depth, LANES)
     whole = pl.BlockSpec(memory_space=pl.ANY)
     vmem = pl.BlockSpec(memory_space=pltpu.VMEM)
     gradient = pl.pallas_call(
@@ -490,19 +491,19 @@
             pltpu.VMEM(units, BF16),
             pltpu.VMEM(units, BF16),
             pltpu.VMEM((groups, slots, tiles) + piece, BF16),
-            pltpu.VMEM((groups, 2, tiles) + piece, BF16),
-            pltpu.VMEM((groups, 2, tiles) + piece, BF16),
-            pltpu.VMEM(units, BF16),
-            pltpu.VMEM(units, BF16),
-            pltpu.VMEM(units, BF16),
-            pltpu.VMEM(units, BF16),
-            pltpu.VMEM(units, BF16),
-            pltpu.VMEM((tiles, depth, LANES), BF16),
-            pltpu.VMEM((tiles, depth, LANES), BF16),
+            pltpu.VMEM((2,) + columns, BF16),
+            pltpu.VMEM((2,) + columns, BF16),
+            pltpu.VMEM(columns, BF16),
+            pltpu.VMEM(columns, BF16),
+            pltpu.VMEM(columns, BF16),
+            pltpu.VMEM(columns, BF16),
+            pltpu.VMEM(columns, BF16),
+            pltpu.VMEM(columns, BF16),
+            pltpu.VMEM(columns, BF16),
             pltpu.SemaphoreType.DMA((4, groups, tiles)),
             pltpu.SemaphoreType.DMA((4, groups, tiles)),
-            pltpu.SemaphoreType.DMA((6, groups)),
-            pltpu.SemaphoreType.DMA((6, groups)),
+            pltpu.SemaphoreType.DMA((6, groups, tiles)),
+            pltpu.SemaphoreType.DMA((6, groups, tiles)),
             pltpu.SemaphoreType.DMA((3, members // slots)),
             pltpu.SemaphoreType.DMA((3, members // slots)),
             pltpu.SemaphoreType.DMA((2,)),

time: 65 us -> 61.7 us (0.949)
  Pallas kernels: 64.8 us -> 61.5 us
    pallas_call x1, Pallas kernels: 62.6 us -> 59.3 us  [per_device(): pl.pallas_call(functools.partial(kernel, slots, tiles, rows, groups), out...]
where the time goes in v5:
time: 61.7 us; the launch traced here: 61.5 us
  Pallas kernels  61.5 us (100%)
    pallas_call x1, Pallas kernels, per_device(): pl.pallas_call(functools.partial(kernel, slots, tiles, rows, groups), out...  59.3 us
    pallas_call x1, Pallas kernels, per_device(): pl.pallas_call(store_kernel, out_shape=jax.ShapeDtypeStruct(gradient.shap...  2.21 us

profile of v5, /device:TPU:0, one launch (start us, length us, event | category | flops | bytes accessed | tf_op | source)
XLA Modules:
  0.0 61.5 jit_solution(17659130325072274765)
XLA Ops:
  0.0 59.3 %shard_map.109.src = bf16[32,160,128]{2,1,0:T(8,128)(2,1)} custom-call(bf16[32,160,128]{2,1,0:T(8,128)(2,1)} %bitcast.4, s32[160,128]{1,0:T(8,128)} %bitcast.6, s32[4,32]{1,0:T(4,128)} %tile_id.1, f32[16,80]{1,0:T(8,128)} %tile_scale.1, bf16[128,128]{1,0:T(8,128)(2,1)} %inv_x.1, bf16[16,16]{1,0:T(8,128)(2,1)} %inv_y.1, bf16[80,80]{1,0:T(8,128)(2,1)} %inv_z.1, ...), custom_call_target="tpu_custom_call" | custom-call | tf_op jit(solution)/shard_map/pallas_call | solution.py:472
  59.3 2.2 %shard_map.110 = bf16[32,160,128]{2,1,0:T(8,128)(2,1)} custom-call(bf16[32,160,128]{2,1,0:T(8,128)(2,1)} %shard_map.109.src), custom_call_target="tpu_custom_call" | custom-call | tf_op jit(solution)/shard_map/pallas_call | solution.py:527

commit v6 on v5

--- a/solution.py
+++ b/solution.py
@@ -168,20 +168,23 @@
     def copy_e(n):
         return to_tile(3, 0, n, stage_e.at[target(n)], recv_e.at[h])
 
+    def two(n):
+        return pl.ds(2 * n, 2)
+
     def copy_far(g, n):
-        return to_slot(0, g, n, spread.at[g, s, n], spread.at[g, s, n], far)
+        return to_slot(0, g, n, spread.at[g, s, two(n)], spread.at[g, s, two(n)], far)
 
     def copy_core(g, n):
-        return to_slot(1, g, n, spread.at[g, s, n], spread.at[g, s, n], sib)
+        return to_slot(1, g, n, spread.at[g, s, two(n)], spread.at[g, s, two(n)], sib)
 
     def copy_on(g, n):
-        return to_slot(2, g, n, spread.at[g, far, n], spread.at[g, far, n], sib)
+        return to_slot(2, g, n, spread.at[g, far, two(n)], spread.at[g, far, two(n)], sib)
 
     def copy_sum(i, n):
-        return to_slot(3 + i, 0, n, stage_c.at[i, n], recv_c.at[i, n], sib)
+        return to_slot(3 + i, 0, n, stage_c.at[i, two(n)], recv_c.at[i, two(n)], sib)
 
     def copy_x(n):
-        return to_slot(5, 0, n, stage_x.at[n], recv_x.at[n], far)
+        return to_slot(5, 0, n, stage_x.at[two(n)], recv_x.at[two(n)], far)
 
     def copy_last(phase, n, m, peer):
         return pltpu.make_async_remote_copy(
@@ -298,39 +301,40 @@
             c = lax.rem(unit, blocks)
             inc[where, pl.ds(pl.multiple_of(c * LANES, LANES), LANES)] += term
 
-    def gather(g, n):
-        if not isinstance(n, int) or n < others:
-            copy_b(g, n).wait_recv()
+    def gather(g, n, count):
+        for i in range(count):
+            copy_b(g, 2 * n + i).wait_recv()
         copy_far(g, n).start()
         copy_core(g, n).start()
-        add_unit(g, s, n)
+        add_unit(g, s, 2 * n)
+        add_unit(g, s, 2 * n + 1)
 
     def pass_on(g, n):
         copy_far(g, n).wait_recv()
         copy_on(g, n).start()
-        add_unit(g, far, n)
+        add_unit(g, far, 2 * n)
+        add_unit(g, far, 2 * n + 1)
         copy_core(g, n).wait_recv()
-        add_unit(g, sib, n)
+        add_unit(g, sib, 2 * n)
+        add_unit(g, sib, 2 * n + 1)
 
     def finish(g, n):
         copy_on(g, n).wait_recv()
-        add_unit(g, diag, n)
-
+        add_unit(g, diag, 2 * n)
+        add_unit(g, diag, 2 * n + 1)
+
+    pairs = tiles // 2
     for g in range(groups):
-        copy_far(g, others).start()
-        copy_core(g, others).start()
-        add_unit(g, s, others)
-        each(others, lambda n: gather(g, n))
+        each(pairs - 1, lambda n: gather(g, n, 2))
+        gather(g, pairs - 1, 1)
     half = dot(pick_y, inv_y[...]).astype(BF16)
     ky[...] = jnp.where(same_level, dot(half, pick_y, 1, 1), 0.0).astype(BF16)
     half = dot(to_level, inv_z[...]).astype(BF16)
     kz[...] = jnp.where(same, dot(half, to_level, 1, 1), 0.0).astype(BF16)
     for g in range(groups):
-        pass_on(g, others)
-        each(others, lambda n: pass_on(g, n))
+        each(pairs, lambda n: pass_on(g, n))
     for g in range(groups):
-        finish(g, others)
-        each(others, lambda n: finish(g, n))
+        each(pairs, lambda n: finish(g, n))
     adj[...] = sea[...] * ((inc[...] * norm * cell_sum[0] - cell_sum[1]) * norm)
 
     def partial(slot, n):
@@ -340,36 +344,40 @@
     for i, slot in enumerate((diag, sib)):
 
         def to_core(n):
-            stage_c[i, n] = partial(slot, n).astype(BF16)
+            for m in (2 * n, 2 * n + 1):
+                stage_c[i, m] = partial(slot, m).astype(BF16)
             copy_sum(i, n).start()
 
-        each(tiles, to_core)
+        each(pairs, to_core)
 
     def between_chips(n):
         copy_sum(0, n).wait_recv()
-        stage_x[n] = (partial(far, n) + recv_c[0, n].astype(F32)).astype(BF16)
+        for m in (2 * n, 2 * n + 1):
+            stage_x[m] = (partial(far, m) + recv_c[0, m].astype(F32)).astype(BF16)
         copy_x(n).start()
 
-    each(tiles, between_chips)
+    each(pairs, between_chips)
 
     def total(n):
+        value = partial(s, n) + recv_c[1, n].astype(F32) + recv_x[n].astype(F32)
+        return value.astype(BF16)
+
+    def exchange(n, count):
         copy_sum(1, n).wait_recv()
         copy_x(n).wait_recv()
-        value = partial(s, n) + recv_c[1, n].astype(F32) + recv_x[n].astype(F32)
-        return value.astype(BF16)
-
-    def exchange(n):
-        stage_d[n] = total(n)
-        copy_d(n).start()
-
-    each(others, exchange)
+        for m in [2 * n, 2 * n + 1][:count]:
+            stage_d[m] = total(m)
+            copy_d(m).start()
+
+    each(pairs - 1, lambda n: exchange(n, 2))
+    exchange(pairs - 1, 1)
     recv_d[h] = total(others)
 
     for g in range(groups):
         each(others, lambda n: copy_a(g, n).wait_send())
         each(others, lambda n: copy_b(g, n).wait_send())
         for copy in (copy_far, copy_core, copy_on):
-            each(tiles, lambda n: copy(g, n).wait_send())
+            each(pairs, lambda n: copy(g, n).wait_send())
 
     def adjoint_z(u):
         deep[u] = dot(kz[...], recv_d[u]).astype(BF16)
@@ -386,6 +394,9 @@
         stage_e[:, where, :] = dot(ky[...], some).astype(BF16).reshape(tiles, GROUP, LANES)
     each(others, lambda n: copy_e(n).start())
     recv_e[h] = stage_e[h]
+    each(others, lambda n: copy_d(n).wait_send())
+    for copy in (lambda n: copy_sum(0, n), lambda n: copy_sum(1, n), copy_x):
+        each(pairs, lambda n: copy(n).wait_send())
 
     def member(n):
         if blocks > 1:
@@ -415,10 +426,7 @@
     for n in turns:
         copy_last(0, n, s * own + member(n), far).wait_recv()
         copy_last(2, n, far * own + member(n), sib).start()
-    each(others, lambda n: copy_d(n).wait_send())
     each(others, lambda n: copy_e(n).wait_send())
-    for copy in (lambda n: copy_sum(0, n), lambda n: copy_sum(1, n), copy_x):
-        each(tiles, lambda n: copy(n).wait_send())
     for n in turns:
         for phase, slot, peer in ((0, s, far), (1, s, sib), (2, far, sib)):
             copy = copy_last(phase, n, slot * own + member(n), peer)
@@ -461,7 +469,7 @@
     members, levels, rows, cols = control.shape
     depth = levels * rows
     blocks = cols // LANES
-    assert slots == 4 and cols % LANES == 0 and cols & (cols - 1) == 0
+    assert slots == 4 and tiles % 2 == 0 and cols % LANES == 0 and cols & (cols - 1) == 0
     assert members // slots * blocks == tiles and depth % GROUP == 0 and 4 % rows == 0
     groups = next(n for n in (2, 1) if depth % (n * GROUP) == 0)
     piece = (depth // groups, LANES)

time: 61.7 us -> 63.3 us (1.026)
  Pallas kernels: 61.5 us -> 63.1 us
    pallas_call x1, Pallas kernels: 59.3 us -> 60.9 us  [per_device(): pl.pallas_call(functools.partial(kernel, slots, tiles, rows, groups), out...]
where the time goes in v6:
time: 63.3 us; the launch traced here: 63.1 us
  Pallas kernels  63.1 us (100%)
    pallas_call x1, Pallas kernels, per_device(): pl.pallas_call(functools.partial(kernel, slots, tiles, rows, groups), out...  60.9 us
    pallas_call x1, Pallas kernels, per_device(): pl.pallas_call(store_kernel, out_shape=jax.ShapeDtypeStruct(gradient.shap...  2.21 us

profile of v6, /device:TPU:0, one launch (start us, length us, event | category | flops | bytes accessed | tf_op | source)
XLA Modules:
  0.0 63.1 jit_solution(3839766074481697045)
XLA Ops:
  0.0 60.9 %shard_map.109.src = bf16[32,160,128]{2,1,0:T(8,128)(2,1)} custom-call(bf16[32,160,128]{2,1,0:T(8,128)(2,1)} %bitcast.4, s32[160,128]{1,0:T(8,128)} %bitcast.6, s32[4,32]{1,0:T(4,128)} %tile_id.1, f32[16,80]{1,0:T(8,128)} %tile_scale.1, bf16[128,128]{1,0:T(8,128)(2,1)} %inv_x.1, bf16[16,16]{1,0:T(8,128)(2,1)} %inv_y.1, bf16[80,80]{1,0:T(8,128)(2,1)} %inv_z.1, ...), custom_call_target="tpu_custom_call" | custom-call | tf_op jit(solution)/shard_map/pallas_call | solution.py:480
  60.9 2.2 %shard_map.110 = bf16[32,160,128]{2,1,0:T(8,128)(2,1)} custom-call(bf16[32,160,128]{2,1,0:T(8,128)(2,1)} %shard_map.109.src), custom_call_target="tpu_custom_call" | custom-call | tf_op jit(solution)/shard_map/pallas_call | solution.py:535
